TPU v7x, 32 devices: a whole 2x2x4 slice. The times are simulated.
32 devices in a mesh: dp: 8 (over z, x), fsdp: 4 (over y, core).
Axes of the slice: x: 2, y: 2, z: 4, core: 2. Of those that a mesh axis runs over, the one named last changes fastest.
Arguments:
- frames: bfloat16 [8, 4, 576, 1024], P('dp', 'fsdp'), may hold values from -6 to 6
- route: int32 [8, 4, 576], P('dp', 'fsdp'), may hold values from 0 to 575, each once within a row
- valid: int32 [8, 4, 576], P('dp', 'fsdp'), may hold values 0 or 1
- w_pw: bfloat16 [1024, 2048], P('fsdp'), may hold values from -0.1875 to 0.1875
- cotangent: bfloat16 [8, 4, 576, 1024], P('dp', 'fsdp'), may hold values from -6 to 6
Outputs:
- gated: bfloat16 [8, 4, 576, 1024], P('dp', 'fsdp')
- grad_pw: bfloat16 [8, 1024, 2048], P('dp', 'fsdp')
Inputs may be any that keep to these rules, and one draw needn't show every extreme that they name: Each row of route is a permutation of the frames of one device.
All inputs are finite; a program needn't handle non-finite values. No bound on the sum of `valid` on one device may be relied on, other than what follows from the above.
Results may differ from a plain program's by a relative error of at most 0.017.
Values may be sent and summed in bfloat16 or wider, within the bound.
A program may use at most 64 MiB of HBM per device.

v0:
```python
import jax
import jax.numpy as jnp
from jax import lax
from jax.sharding import PartitionSpec as P


def per_device(frames, route, valid, w_pw, cotangent):
    width = frames.shape[3]
    local = frames[0, 0]
    order = route[0, 0]
    picked = jnp.take(local, order, axis=0)
    keep = jnp.take(valid[0, 0], order, axis=0)
    sent = jnp.where(keep[:, None] > 0, picked, jnp.zeros_like(picked))
    received = lax.all_to_all(sent, "dp", split_axis=0, concat_axis=0, tiled=True)
    values = received.astype(jnp.float32)
    mean = jnp.mean(values, axis=-1, keepdims=True)
    centred = values - mean
    variance = jnp.mean(centred * centred, axis=-1, keepdims=True)
    normed = (centred * lax.rsqrt(variance + 1e-05)).astype(jnp.bfloat16)
    columns = normed
    pre = jnp.dot(
        columns,
        lax.all_gather(w_pw, "fsdp", axis=0, tiled=True),
        preferred_element_type=jnp.float32,
    )
    first = pre[:, :width]
    second = jax.nn.sigmoid(pre[:, width:])
    gated = (first * second).astype(jnp.bfloat16)
    upstream = cotangent[0, 0].astype(jnp.float32)
    dpre = jnp.concatenate(
        [upstream * second, upstream * first * second * (1.0 - second)], axis=1
    ).astype(jnp.bfloat16)
    columns = normed
    grad_share = lax.psum_scatter(
        lax.dot_general(
            columns, dpre, (((0,), (0,)), ((), ())), preferred_element_type=jnp.float32
        ).astype(jnp.bfloat16),
        "fsdp",
        scatter_dimension=0,
        tiled=True,
    )
    return (gated[None, None], grad_share[None])


def solution(mesh):
    in_specs = (
        P("dp", "fsdp", None, None),
        P("dp", "fsdp", None),
        P("dp", "fsdp", None),
        P("fsdp", None),
        P("dp", "fsdp", None, None),
    )
    out_specs = (P("dp", "fsdp", None, None), P("dp", "fsdp", None))
    return jax.shard_map(
        per_device, mesh=mesh, in_specs=in_specs, out_specs=out_specs, check_vma=False
    )
```

profile of v0, /device:TPU:10, one launch (start us, length us, event | category | flops | bytes accessed | tf_op | source)
XLA Modules:
  0.0 114.0 jit_solution(7613696907484949976)
XLA Ops:
  7.2 0.0 copy-start
  7.2 0.0 all-gather.2.cloned.1.call-start
  7.2 0.7 all-gather.2.cloned.1.call-update
  7.9 0.0 reduce-scatter.2.cloned.1.call-start
  8.0 0.7 reduce.3
  8.7 0.7 reduce.2
  9.4 0.7 fusion.13
  10.1 2.6 %gather_fusion = s32[576]{0:T(1024)S(1)} fusion(s32[576]{0:T(1024)S(1)} %reduce.3, s32[1024]{0:T(1024)S(1)} %pad_clamp_fusion), kind=kCustom, calls=%fused_computation | custom fusion | bytes 6912 | tf_op jit(solution)/shard_map/jit(_take)/gather | solution.py:12
  12.7 0.1 gather.13
  12.7 0.1 squeeze.12
  12.8 0.0 copy-done
  12.8 2.9 %gather_fusion.1 = bf16[576,1024]{1,0:T(8,128)(2,1)S(1)} fusion(bf16[576,1024]{1,0:T(8,128)(2,1)S(1)} %bitcast.20, s32[1024]{0:T(1024)S(1)} %pad_clamp_fusion), kind=kCustom, calls=%fused_computation.1 | custom fusion | bytes 2361600 | tf_op jit(solution)/shard_map/jit(_take)/gather | solution.py:11
  15.7 0.2 select_select_fusion
  16.0 32.8 %all_to_all.6 = bf16[8,72,1024]{2,1,0:T(8,128)(2,1)S(1)} all-to-all(bf16[8,72,1024]{2,1,0:T(8,128)(2,1)S(1)} %select_select_fusion), channel_id=1, replica_groups=mesh['dp'=8,'fsdp'=4] {'dp'}, dimensions={0} | all-to-all | bytes 2359296 | tf_op jit(solution)/shard_map/all_to_all | solution.py:14
  48.7 0.2 convert_reduce_fusion
  49.0 0.1 div.12
  49.1 0.5 multiply_reduce_fusion
  49.6 0.1 rsqrt.12
  49.6 0.3 fusion.11
  50.0 0.0 copy-start.1
  50.0 0.0 all-gather.2.cloned.1.call-done
  50.0 4.5 %fusion.15 = f32[576,2048]{1,0:T(8,128)S(1)} fusion(bf16[576,1024]{1,0:T(8,128)(2,1)S(1)} %fusion.11, bf16[1024,2048]{1,0:T(8,128)(2,1)} %all-gather.2.cloned.1.call-done), kind=kOutput, calls=%fused_computation.33 | convolution fusion | flops 2415919104 | bytes 10092544 | tf_op jit(solution)/shard_map/dot_general | solution.py:21
  54.5 0.0 copy-done.1
  54.5 2.4 %fusion = (bf16[576,1024]{1,0:T(8,128)(2,1)S(1)}, bf16[576,1024]{1,0:T(8,128)(2,1)S(1)}, bf16[1,1,576,1024]{3,2,1,0:T(8,128)(2,1)}) fusion(bf16[1,1,576,1024]{3,2,1,0:T(8,128)(2,1)S(1)} %copy-done.1, f32[576,2048]{1,0:T(8,128)S(1)} %fusion.15), kind=kLoop, calls=%fused_computation.5 | loop fusion | flops 7667712 | bytes 9437184 | tf_op jit(solution)/shard_map/convert.2
  56.9 5.2 %convolution_convert_fusion = bf16[1024,2048]{1,0:T(8,128)(2,1)} fusion(bf16[576,1024]{1,0:T(8,128)(2,1)S(1)} %fusion.11, bf16[576,1024]{1,0:T(8,128)(2,1)S(1)} %get-tuple-element.5, bf16[576,1024]{1,0:T(8,128)(2,1)S(1)} %get-tuple-element.4), kind=kOutput, calls=%fused_computation.2 | convolution fusion | flops 2422734848 | bytes 7733248 | tf_op jit(solution)/shard_map/dot_general | solution.py:35
  62.1 0.0 reduce-scatter.2.cloned.1.call-update
  62.1 45.0 %reduce-scatter.2.cloned.1.call-done = bf16[256,2048]{1,0:T(8,128)(2,1)} async-done(((bf16[1024,2048]{1,0:T(8,128)(2,1)}), bf16[256,2048]{1,0:T(8,128)(2,1)}) %reduce-scatter.2.cloned.1.call-update) | async-done | bytes 1048592 | tf_op jit(solution)/shard_map/reduce_scatter | solution.py:34
  (4 shorter events, 0.0 us)
Async XLA Ops:
  7.2 5.7 %copy-start = (bf16[1,1,576,1024]{3,2,1,0:T(8,128)(2,1)S(1)}, bf16[1,1,576,1024]{3,2,1,0:T(8,128)(2,1)}, u32[]{:S(2)}) copy-start(bf16[1,1,576,1024]{3,2,1,0:T(8,128)(2,1)} %param.5) | copy-start | bytes 3538948
  7.2 42.8 %all-gather.2.cloned.1.call-start = ((), (), s32[]{:S(2)}) async-start(), calls=%async_computation.2 | async-start | bytes 5242880 | tf_op jit(solution)/shard_map/all_gather | solution.py:23
  7.9 99.2 %reduce-scatter.2.cloned.1.call-start = ((), (), s32[]{:S(2)}) async-start(), calls=%async_computation.3 | async-start | bytes 5242880 | tf_op jit(solution)/shard_map/reduce_scatter | solution.py:34
  50.0 4.5 %copy-start.1 = (bf16[1,1,576,1024]{3,2,1,0:T(8,128)(2,1)S(1)}, bf16[1,1,576,1024]{3,2,1,0:T(8,128)(2,1)}, u32[]{:S(2)}) copy-start(bf16[1,1,576,1024]{3,2,1,0:T(8,128)(2,1)} %param.9) | copy-start | bytes 3538948
Sparse Core Ops, SparseCore 0:
  9.6 35.6 all-gather.1
  62.2 44.8 reduce-scatter.1
where the time goes:
time: 116 us; the launch traced here: 114 us
  waiting for transfers between devices  45.7 us (39%)
  blocking collectives  32.8 us (28%)
  between operations  14.1 us (12%)
  matrix products  9.67 us (8%)
  other arithmetic  5.81 us (5%)
  local copies, waits for them, and re-layouts  5.76 us (5%)
    reduce_scatter x1, waiting for transfers between devices, per_device(): lax.psum_scatter(lax.dot_general(columns, dpre, (((0,), (0,)), ((), ())),...  45 us
    all_to_all x1, blocking collectives, per_device(): lax.all_to_all(sent, 'dp', split_axis=0, concat_axis=0, tiled=True)  32.8 us
    dot_general x1, matrix products, per_device(): lax.dot_general(columns, dpre, (((0,), (0,)), ((), ())), preferred_elemen...  5.18 us
    dot_general x1, matrix products, per_device(): jnp.dot(columns, lax.all_gather(w_pw, 'fsdp', axis=0, tiled=True), prefer...  4.49 us
    gather x1, local copies, waits for them, and re-layouts, per_device(): picked = jnp.take(local, order, axis=0)  2.87 us
    gather x2, local copies, waits for them, and re-layouts, per_device(): keep = jnp.take(valid[0, 0], order, axis=0)  2.66 us
    another operation x1, other arithmetic  2.38 us
  transfers between devices with their start and end apart: 2, of which 1 were waited for; matrix products, arithmetic and copies ran while one was open for 8% of the time, Pallas kernels for 0%

commit v1 on v0

--- a/solution.py
+++ b/solution.py
@@ -1,10 +1,17 @@
+import functools
+
 import jax
 import jax.numpy as jnp
 from jax import lax
+from jax.experimental import pallas as pl
+from jax.experimental.pallas import tpu as pltpu
 from jax.sharding import PartitionSpec as P
 
-
-def per_device(frames, route, valid, w_pw, cotangent):
+TILE = 256
+W_PARTS = 4
+
+
+def plain(frames, route, valid, w_pw, cotangent):
     width = frames.shape[3]
     local = frames[0, 0]
     order = route[0, 0]
@@ -17,9 +24,8 @@
     centred = values - mean
     variance = jnp.mean(centred * centred, axis=-1, keepdims=True)
     normed = (centred * lax.rsqrt(variance + 1e-05)).astype(jnp.bfloat16)
-    columns = normed
     pre = jnp.dot(
-        columns,
+        normed,
         lax.all_gather(w_pw, "fsdp", axis=0, tiled=True),
         preferred_element_type=jnp.float32,
     )
@@ -30,10 +36,9 @@
     dpre = jnp.concatenate(
         [upstream * second, upstream * first * second * (1.0 - second)], axis=1
     ).astype(jnp.bfloat16)
-    columns = normed
     grad_share = lax.psum_scatter(
         lax.dot_general(
-            columns, dpre, (((0,), (0,)), ((), ())), preferred_element_type=jnp.float32
+            normed, dpre, (((0,), (0,)), ((), ())), preferred_element_type=jnp.float32
         ).astype(jnp.bfloat16),
         "fsdp",
         scatter_dimension=0,
@@ -42,7 +47,261 @@
     return (gated[None, None], grad_share[None])
 
 
+def kernel(
+    n_dp, n_fsdp,
+    frames_ref, route_ref, valid_ref, w_ref, cot_ref, gated_ref, grad_ref,
+    frames_v, route_v, valid_v, cot_v, gated_v, out_v,
+    sent, recv, normed, turned, w_all, dpre,
+    mate_out, mate_in, peer_out, peer_in, own_out, own_in, own_sum,
+    load_sem, self_sem, a2a_send, a2a_recv,
+    w_send, w_recv, wm_send, wm_recv, wf_send, wf_recv,
+    m_send, m_recv, p_send, p_recv, o_send, o_recv, g_sem, d_sem,
+):
+    f32, bf16 = jnp.float32, jnp.bfloat16
+    me = lax.axis_index("dp")
+    f = lax.axis_index("fsdp")
+    mate = f + 1 - 2 * lax.rem(f, 2)
+    peer = lax.rem(f + 2, n_fsdp)
+    peer_mate = lax.rem(mate + 2, n_fsdp)
+    rows, width = frames_v.shape
+    block = rows // n_dp
+    shard = w_ref.shape[0]
+    part = shard // W_PARTS
+    tiles = width // TILE
+
+    barrier = pltpu.get_barrier_semaphore()
+    for k in range(1, n_dp):
+        pl.semaphore_signal(barrier, inc=1, device_id={"dp": lax.rem(me + k, n_dp)})
+    pl.semaphore_signal(barrier, inc=1, device_id={"fsdp": mate})
+    pl.semaphore_signal(barrier, inc=1, device_id={"fsdp": peer})
+
+    loads = [
+        pltpu.make_async_copy(route_ref, route_v, load_sem.at[0]),
+        pltpu.make_async_copy(valid_ref, valid_v, load_sem.at[1]),
+        pltpu.make_async_copy(frames_ref, frames_v, load_sem.at[2]),
+        pltpu.make_async_copy(w_ref, w_all.at[pl.ds(pl.multiple_of(f * shard, shard), shard)], load_sem.at[3]),
+        pltpu.make_async_copy(cot_ref, cot_v, load_sem.at[4]),
+    ]
+    for load in loads:
+        load.start()
+
+    def w_rows(owner, i):
+        return pl.ds(pl.multiple_of(owner * shard + i * part, part), part)
+
+    def w_to_peer(i):
+        return pltpu.make_async_remote_copy(
+            w_ref.at[pl.ds(i * part, part)], w_all.at[w_rows(f, i)],
+            w_send.at[i], w_recv.at[i], device_id={"fsdp": peer})
+
+    def w_to_mate(i):
+        return pltpu.make_async_remote_copy(
+            w_ref.at[pl.ds(i * part, part)], w_all.at[w_rows(f, i)],
+            wm_send.at[i], wm_recv.at[i], device_id={"fsdp": mate})
+
+    def w_onward(i):
+        return pltpu.make_async_remote_copy(
+            w_all.at[w_rows(peer, i)], w_all.at[w_rows(peer, i)],
+            wf_send.at[i], wf_recv.at[i], device_id={"fsdp": mate})
+
+    pl.semaphore_wait(barrier, n_dp + 1)
+    for i in range(W_PARTS):
+        w_to_peer(i).start()
+    for i in range(W_PARTS):
+        w_to_mate(i).start()
+
+    for load in loads[:2]:
+        load.wait()
+    route = route_v[...]
+    hit = lax.broadcasted_iota(jnp.int32, (rows, rows), 0) == route
+    pick = jnp.where(hit, 1.0, 0.0).astype(bf16)
+    real = jnp.where(valid_v[...] > 0, 1.0, 0.0).astype(bf16)
+    keep = jnp.dot(jnp.broadcast_to(real, (16, rows)), pick, preferred_element_type=f32)[:1]
+    pick = jnp.where(hit, keep, 0.0).astype(bf16)
+    loads[2].wait()
+    picked = lax.dot_general(
+        pick, frames_v[...], (((0,), (0,)), ((), ())), preferred_element_type=f32)
+    for t in range(n_dp):
+        sent[t] = picked[t * block:(t + 1) * block].astype(bf16)
+
+    def to_trainer(k):
+        t = lax.rem(me + k, n_dp)
+        return pltpu.make_async_remote_copy(
+            sent.at[t], recv.at[me], a2a_send.at[t], a2a_recv.at[me], device_id={"dp": t})
+
+    order = sorted(range(1, n_dp), key=lambda k: -min(k, n_dp - k))
+    for k in order:
+        to_trainer(k).start()
+    stay = pltpu.make_async_copy(sent.at[me], recv.at[me], self_sem)
+    stay.start()
+    stay.wait()
+
+    pairs = n_dp // 2
+
+    def norm_pair(j):
+        pair = lax.rem(me // 2 + j, pairs)
+        for half in range(2):
+            s = 2 * pair + half
+
+            @pl.when(s != me)
+            def _():
+                pltpu.make_async_remote_copy(
+                    sent.at[s], recv.at[s], a2a_send.at[s], a2a_recv.at[s], device_id={"dp": s}
+                ).wait_recv()
+
+        values = jnp.concatenate([recv[2 * pair].astype(f32), recv[2 * pair + 1].astype(f32)], axis=0)
+        mean = jnp.mean(values, axis=-1, keepdims=True)
+        centred = values - mean
+        variance = jnp.mean(centred * centred, axis=-1, keepdims=True)
+        at = pl.ds(pl.multiple_of(pair * 2 * block, 2 * block), 2 * block)
+        normed[at, :] = (centred * lax.rsqrt(variance + 1e-05)).astype(bf16)
+
+    for j in range(max(pairs, W_PARTS)):
+        if j < W_PARTS:
+            w_to_peer(j).wait_recv()
+            w_onward(j).start()
+        if j < pairs:
+            norm_pair(j)
+    for q in range(n_fsdp):
+        turned[q] = normed[:, q * shard:(q + 1) * shard].T
+
+    loads[3].wait()
+    loads[4].wait()
+    for i in range(W_PARTS):
+        w_to_mate(i).wait_recv()
+    for i in range(W_PARTS):
+        w_onward(i).wait_recv()
+
+    def mate_copy(i):
+        return pltpu.make_async_remote_copy(
+            mate_out.at[i], mate_in.at[i], m_send.at[i], m_recv.at[i], device_id={"fsdp": mate})
+
+    def own_copy(i):
+        return pltpu.make_async_remote_copy(
+            own_out.at[i], own_in.at[i], o_send.at[i], o_recv.at[i], device_id={"fsdp": mate})
+
+    def peer_copy(i):
+        return pltpu.make_async_remote_copy(
+            peer_out.at[i], peer_in.at[i], p_send.at[i], p_recv.at[i], device_id={"fsdp": peer})
+
+    def gated_copy(i):
+        cols = pl.ds(pl.multiple_of(i * TILE, TILE), TILE)
+        return pltpu.make_async_copy(gated_v.at[:, cols], gated_ref.at[:, cols], g_sem.at[i])
+
+    def partial(q):
+        return jnp.dot(turned[q], dpre[...], preferred_element_type=f32)
+
+    def tile(i, carry):
+        lo = pl.ds(pl.multiple_of(i * TILE, TILE), TILE)
+        hi = pl.ds(pl.multiple_of(width + i * TILE, TILE), TILE)
+        rows_in = normed[...]
+        first = jnp.dot(rows_in, w_all[:, lo], preferred_element_type=f32)
+        second = jax.nn.sigmoid(jnp.dot(rows_in, w_all[:, hi], preferred_element_type=f32))
+        upstream = cot_v[:, lo].astype(f32)
+        gated_v[:, lo] = (first * second).astype(bf16)
+        dpre[:, :TILE] = (upstream * second).astype(bf16)
+        dpre[:, TILE:] = (upstream * first * second * (1.0 - second)).astype(bf16)
+        gated_copy(i).start()
+        mate_out[i] = partial(peer_mate).astype(bf16)
+        mate_copy(i).start()
+        chip_sum = partial(peer)
+        own_out[i] = partial(mate).astype(bf16)
+        own_copy(i).start()
+        own_sum[i] = partial(f)
+        mate_copy(i).wait_recv()
+        peer_out[i] = (chip_sum + mate_in[i].astype(f32)).astype(bf16)
+        peer_copy(i).start()
+        return carry
+
+    lax.fori_loop(0, tiles, tile, 0)
+
+    def grad_copies(i):
+        lo = pl.ds(pl.multiple_of(i * TILE, TILE), TILE)
+        hi = pl.ds(pl.multiple_of(width + i * TILE, TILE), TILE)
+        return (
+            pltpu.make_async_copy(out_v.at[i, :, pl.ds(0, TILE)], grad_ref.at[:, lo], d_sem.at[i, 0]),
+            pltpu.make_async_copy(out_v.at[i, :, pl.ds(TILE, TILE)], grad_ref.at[:, hi], d_sem.at[i, 1]),
+        )
+
+    def finish(i, carry):
+        own_copy(i).wait_recv()
+        half = own_sum[i] + own_in[i].astype(f32)
+        peer_copy(i).wait_recv()
+        out_v[i] = (half + peer_in[i].astype(f32)).astype(bf16)
+        for copy in grad_copies(i):
+            copy.start()
+        return carry
+
+    lax.fori_loop(0, tiles, finish, 0)
+
+    for k in order:
+        to_trainer(k).wait_send()
+    for i in range(W_PARTS):
+        w_to_peer(i).wait_send()
+        w_to_mate(i).wait_send()
+        w_onward(i).wait_send()
+
+    def drain(i, carry):
+        gated_copy(i).wait()
+        mate_copy(i).wait_send()
+        own_copy(i).wait_send()
+        peer_copy(i).wait_send()
+        for copy in grad_copies(i):
+            copy.wait()
+        return carry
+
+    lax.fori_loop(0, tiles, drain, 0)
+
+
+def fused(n_dp, n_fsdp, frames, route, valid, w_pw, cotangent):
+    rows, width = frames.shape[2:]
+    shard, wide = w_pw.shape
+    block, tiles = rows // n_dp, width // TILE
+    bf16, f32, i32 = jnp.bfloat16, jnp.float32, jnp.int32
+    chunk = (tiles, shard, 2 * TILE)
+    dma = pltpu.SemaphoreType.DMA
+    scratch = [
+        pltpu.VMEM((rows, width), bf16), pltpu.VMEM((1, rows), i32), pltpu.VMEM((1, rows), i32),
+        pltpu.VMEM((rows, width), bf16), pltpu.VMEM((rows, width), bf16), pltpu.VMEM(chunk, bf16),
+        pltpu.VMEM((n_dp, block, width), bf16), pltpu.VMEM((n_dp, block, width), bf16),
+        pltpu.VMEM((rows, width), bf16), pltpu.VMEM((n_fsdp, shard, rows), bf16),
+        pltpu.VMEM((width, wide), bf16), pltpu.VMEM((rows, 2 * TILE), bf16),
+        *[pltpu.VMEM(chunk, bf16) for _ in range(6)], pltpu.VMEM(chunk, f32),
+        dma((5,)), dma, dma((n_dp,)), dma((n_dp,)),
+        *[dma((W_PARTS,)) for _ in range(6)],
+        *[dma((tiles,)) for _ in range(7)], dma((tiles, 2)),
+    ]
+    macs = rows * width * wide * 2 + rows * rows * width
+    gated, grad = pl.pallas_call(
+        functools.partial(kernel, n_dp, n_fsdp),
+        out_shape=(
+            jax.ShapeDtypeStruct((rows, width), bf16),
+            jax.ShapeDtypeStruct((shard, wide), bf16),
+        ),
+        in_specs=[pl.BlockSpec(memory_space=pl.ANY)] * 5,
+        out_specs=[pl.BlockSpec(memory_space=pl.ANY)] * 2,
+        scratch_shapes=scratch,
+        cost_estimate=pl.CostEstimate(
+            flops=2 * macs, bytes_accessed=(3 * rows * width + 2 * shard * wide) * 2,
+            transcendentals=rows * width),
+        compiler_params=pltpu.CompilerParams(
+            collective_id=0, has_side_effects=True, vmem_limit_bytes=50 * 1024 * 1024),
+    )(frames[0, 0], route[0], valid[0], w_pw, cotangent[0, 0])
+    return (gated[None, None], grad[None])
+
+
 def solution(mesh):
+    n_dp, n_fsdp = mesh.shape["dp"], mesh.shape["fsdp"]
+
+    def per_device(frames, route, valid, w_pw, cotangent):
+        rows, width = frames.shape[2:]
+        fits = (
+            n_fsdp == 4 and n_dp % 2 == 0 and rows % (8 * n_dp) == 0
+            and width % (n_fsdp * TILE) == 0 and w_pw.shape[0] % (16 * W_PARTS) == 0
+        )
+        if fits:
+            return fused(n_dp, n_fsdp, frames, route, valid, w_pw, cotangent)
+        return plain(frames, route, valid, w_pw, cotangent)
+
     in_specs = (
         P("dp", "fsdp", None, None),
         P("dp", "fsdp", None),

time: 116 us -> 67.3 us (0.58); the launches traced: 114 us -> 67.1 us
  Pallas kernels: 0 us -> 61.9 us
  waiting for transfers between devices: 45.7 us -> 0 us
  blocking collectives: 32.8 us -> 0 us
  between operations: 14.1 us -> 0.65 us
  matrix products: 9.67 us -> 0 us
  other arithmetic: 5.81 us -> 0 us
  local copies, waits for them, and re-layouts: 5.76 us -> 4.57 us
    pallas_call x0 -> x1, Pallas kernels: none -> 61.9 us  [fused(): pl.pallas_call(functools.partial(kernel, n_dp, n_fsdp), out_shape=(jax.Sh...]
    reduce_scatter x1 -> x0, waiting for transfers between devices: 45 us -> none  [per_device(): lax.psum_scatter(lax.dot_general(columns, dpre, (((0,), (0,)), ((), ())),...]
    all_to_all x1 -> x0, blocking collectives: 32.8 us -> none  [per_device(): lax.all_to_all(sent, 'dp', split_axis=0, concat_axis=0, tiled=True)]
    dot_general x2 -> x0, matrix products: 9.67 us -> none  [the longest x1 5.18 us: per_device(): lax.dot_general(columns, dpre, (((0,), (0,)), ((), ())), preferred_elemen...]
    gather x3 -> x0, local copies, waits for them, and re-layouts: 5.53 us -> none  [the longest x1 2.87 us: per_device(): picked = jnp.take(local, order, axis=0)]
    unnamed x4 -> x8, local copies, waits for them, and re-layouts: 0.02 us -> 4.57 us
    another operation x1 -> x0, other arithmetic: 2.38 us -> none
    unnamed x2 -> x0, other arithmetic: 1.4 us -> none
  transfers between devices with their start and end apart: 2 -> 0, of which waited for: 1 -> 0; matrix products, arithmetic and copies ran while one was open for 8% -> 0% of each run, Pallas kernels for 0% -> 0%
where the time goes in v1:
time: 67.3 us; the launch traced here: 67.1 us
  Pallas kernels  61.9 us (92%)
  local copies, waits for them, and re-layouts  4.57 us (7%)
    pallas_call x1, Pallas kernels, fused(): pl.pallas_call(functools.partial(kernel, n_dp, n_fsdp), out_shape=(jax.Sh...  61.9 us
    unnamed x8, local copies, waits for them, and re-layouts  4.57 us

profile of v1, /device:TPU:10, one launch (start us, length us, event | category | flops | bytes accessed | tf_op | source)
XLA Modules:
  0.0 67.1 jit_solution(8023077097814019364)
XLA Ops:
  0.6 0.0 copy-start
  0.6 1.2 %copy-done = bf16[256,2048]{1,0:T(8,128)(2,1)S(1)} copy-done((bf16[256,2048]{1,0:T(8,128)(2,1)S(1)}, bf16[256,2048]{1,0:T(8,128)(2,1)}, u32[]{:S(2)}) %copy-start) | copy-done | bytes 1048600
  1.9 0.0 copy-start.1
  1.9 0.7 %copy-done.1 = s32[1,1,576]{2,1,0:T(1,128)S(1)} copy-done((s32[1,1,576]{2,1,0:T(1,128)S(1)}, s32[1,1,576]{2,1,0:T(1,128)}, u32[]{:S(2)}) %copy-start.1) | copy-done | bytes 2328
  2.5 0.0 copy-start.2
  2.5 0.7 %copy-done.2 = s32[1,1,576]{2,1,0:T(1,128)S(1)} copy-done((s32[1,1,576]{2,1,0:T(1,128)S(1)}, s32[1,1,576]{2,1,0:T(1,128)}, u32[]{:S(2)}) %copy-start.2) | copy-done | bytes 2328
  3.2 61.9 %shard_map.68 = (bf16[576,1024]{1,0:T(8,128)(2,1)S(1)}, bf16[256,2048]{1,0:T(8,128)(2,1)S(1)}) custom-call(bf16[576,1024]{1,0:T(8,128)(2,1)} %bitcast.10, s32[1,576]{1,0:T(1,128)S(1)} %bitcast.8, s32[1,576]{1,0:T(1,128)S(1)} %bitcast.9, bf16[256,2048]{1,0:T(8,128)(2,1)S(1)} %copy-done, bf16[576,1024]{1,0:T(8,128)(2,1)} %bitcast.11), custom_call_target="tpu_custom_call" | custom-call | flops 5511315456 | bytes 5636096 | tf_op jit(solution)/shard_map/pallas_call | solution.py:274
  65.1 1.0 %copy.9 = bf16[1,1,576,1024]{3,2,1,0:T(8,128)(2,1)} copy(bf16[1,1,576,1024]{3,2,1,0:T(8,128)(2,1)S(1)} %bitcast.6) | data formatting | bytes 2359296
  66.1 1.0 %copy.10 = bf16[1,256,2048]{2,1,0:T(8,128)(2,1)} copy(bf16[1,256,2048]{2,1,0:T(8,128)(2,1)S(1)} %bitcast.7) | data formatting | bytes 2097152
Async XLA Ops:
  0.6 1.2 %copy-start = (bf16[256,2048]{1,0:T(8,128)(2,1)S(1)}, bf16[256,2048]{1,0:T(8,128)(2,1)}, u32[]{:S(2)}) copy-start(bf16[256,2048]{1,0:T(8,128)(2,1)} %w_ref.1) | copy-start | bytes 3145732
  1.9 0.7 %copy-start.1 = (s32[1,1,576]{2,1,0:T(1,128)S(1)}, s32[1,1,576]{2,1,0:T(1,128)}, u32[]{:S(2)}) copy-start(s32[1,1,576]{2,1,0:T(1,128)} %param.6) | copy-start | bytes 6916
  2.5 0.7 %copy-start.2 = (s32[1,1,576]{2,1,0:T(1,128)S(1)}, s32[1,1,576]{2,1,0:T(1,128)}, u32[]{:S(2)}) copy-start(s32[1,1,576]{2,1,0:T(1,128)} %param.7) | copy-start | bytes 6916
